TPU v7x, 128 devices: a whole 4x4x4 slice. The times are simulated.
128 devices in a mesh: ctx: 8 (over y_hi, z), tp: 4 (over x), req: 4 (over y_lo, core).
Axes of the slice: x: 4, y: 4 (y_hi: 2, y_lo: 2; y = y_hi * 2 + y_lo), z: 4, core: 2. Of those that a mesh axis runs over, the one named last changes fastest.
Arguments:
- queries: bfloat16 [256, 8, 8192], P('ctx', 'req', 'tp'), parts along dimension 1, may hold values from -5 to 5
- key_cache: bfloat16 [24576, 8, 512], P('ctx', 'req', 'tp'), parts along dimension 1, may hold values from -10 to 10
- value_cache: bfloat16 [24576, 8, 512], P('ctx', 'req', 'tp'), parts along dimension 1, may hold values from -6 to 6
- ctx_len: int32 [8], P('req'), parts along dimension 0, may hold values from 6080 to 24320, as said below
- new_count: int32 [8], P('req'), parts along dimension 0, may hold values from 64 to 256, as said below
Outputs:
- attended_out: bfloat16 [256, 8, 8192], P(('ctx', 'tp'), 'req'), parts along dimension 1
There are 4 independent parts, one for each index of `req`. A program takes and returns all parts, laid end to end along the dimension named above; each array names one. Nothing has to cross between parts.
Inputs may be any that keep to these rules, and one draw needn't show every extreme that they name: `ctx_len`: some request has exactly 24320 cached tokens. Some request has exactly 256 new tokens; the slots ctx_len to ctx_len + new_count - 1 hold the new tokens' keys and values.
All inputs are finite; a program needn't handle non-finite values.
Results may differ from a plain program's by a relative error of at most 0.0075.
Values may be sent and summed in bfloat16 or wider, within the bound.
No kernel may reach another device: no remote copies, remote signals or barrier semaphores. Data moves between devices by JAX's collectives and lax.ppermute only.
A program may use at most 256 MiB of HBM per device.

v0:
```python
import math

import jax
import jax.numpy as jnp
from jax import lax
from jax.experimental import pallas as pl
from jax.experimental.pallas import tpu as pltpu
from jax.sharding import PartitionSpec as P

HD = 128
NEWQ = 256
TB = 32
KC = 256
HIDDEN = -1e30
RATE = math.log2(math.e) * HD ** (-0.5)
VMEM = pl.BlockSpec(memory_space=pltpu.VMEM)
SMEM = pl.BlockSpec(memory_space=pltpu.SMEM)


def pack_logs(ls, heads):
    lanes = lax.broadcasted_iota(jnp.int32, ls.shape, 1)
    high = ls.astype(jnp.bfloat16).astype(jnp.float32)
    rest = ls - high
    mid = rest.astype(jnp.bfloat16).astype(jnp.float32)
    packed = jnp.where(lanes < heads, high, jnp.where(lanes < 2 * heads, mid, rest - mid))
    return packed.astype(jnp.bfloat16)


def attend_kernel(meta, q_ref, k_ref, vt_ref, o_ref, s, mx):
    slots = k_ref.shape[0]
    width = q_ref.shape[1]
    heads = width // HD
    lanes = heads * TB
    ctx_len, new_count, base = meta[0], meta[1], meta[2]
    edge = ctx_len - base + 1
    some = edge + NEWQ - 1 > 0
    tiles = jnp.where(some, (new_count + TB - 1) // TB, 0)
    of_head = lax.broadcasted_iota(jnp.int32, (TB, HD), 1) % heads
    token = lax.broadcasted_iota(jnp.int32, (1, lanes), 1) % TB
    key = lax.broadcasted_iota(jnp.int32, (KC, lanes), 0)

    @pl.loop(tiles, NEWQ // TB)
    def _(i):
        row = pl.multiple_of(i * TB, TB)
        o_ref[pl.ds(row, TB), :width] = jnp.zeros((TB, width), o_ref.dtype)
        o_ref[pl.ds(row, TB), width:] = pack_logs(jnp.full((TB, HD), HIDDEN, jnp.float32), heads)

    def step(i, span, clear):
        row = pl.multiple_of(jnp.minimum(i, tiles - 1) * TB, TB)
        q = jnp.concatenate(
            [q_ref[pl.ds(row, TB), h * HD:(h + 1) * HD] for h in range(heads)], axis=0)
        shown = edge + row + token
        shift = jnp.max(mx[...], axis=0, keepdims=True) * RATE
        top = acc = total = None
        for c in range(span):
            at = slice(c * KC, (c + 1) * KC)
            e = jnp.exp2(s[at, :] * RATE - shift)
            part = lax.dot_general(k_ref[at, :], q, (((1,), (1,)), ((), ())),
                                   preferred_element_type=jnp.float32)
            if c >= clear:
                part = jnp.where(key < shown - c * KC, part, HIDDEN)
            s[at, :] = part
            high = jnp.max(part.reshape(KC // 8, 8, lanes), axis=0)
            top = high if top is None else jnp.maximum(top, high)
            add = jnp.sum(e.reshape(KC // 8, 8, lanes), axis=0)
            total = add if total is None else total + add
            new = jnp.dot(vt_ref[:, at], e.astype(jnp.bfloat16), preferred_element_type=jnp.float32)
            acc = new if acc is None else acc + new
        mx[...] = top
        row = pl.multiple_of(jnp.maximum(i - 1, 0) * TB, TB)
        total = jnp.sum(total, axis=0, keepdims=True)
        out = (acc / total).T
        ls = jnp.broadcast_to(shift + jnp.log2(total), (HD, lanes)).T
        kept = jnp.zeros((TB, HD), jnp.float32)
        for h in range(heads):
            at = slice(h * TB, (h + 1) * TB)
            o_ref[pl.ds(row, TB), h * HD:(h + 1) * HD] = out[at].astype(o_ref.dtype)
            kept = jnp.where(of_head == h, ls[at], kept)
        o_ref[pl.ds(row, TB), width:] = pack_logs(kept, heads)

    def run(span, clear):
        @pl.loop(0, tiles + 1)
        def _(i):
            step(i, span, clear)

    chunks = slots // KC
    cuts = (0, 3, 7, 10, chunks - 1, chunks)
    for low, high in zip(cuts, cuts[1:] + (None,)):
        span = chunks if high is None else min(chunks, high + NEWQ // KC)
        clear = low
        here = tiles > 0
        if low > 0:
            here = here & (edge >= low * KC)
        if high is not None:
            here = here & (edge < high * KC)

        @pl.when(here)
        def _(span=span, clear=clear):
            run(span, clear)


def attend(meta, q, k, vt):
    rows, width = q.shape
    slots = k.shape[0]
    heads = width // HD
    return pl.pallas_call(
        attend_kernel,
        out_shape=jax.ShapeDtypeStruct((rows, width + HD), jnp.bfloat16),
        in_specs=[SMEM, VMEM, VMEM, VMEM],
        out_specs=VMEM,
        scratch_shapes=[
            pltpu.VMEM((slots, heads * TB), jnp.float32),
            pltpu.VMEM((8, heads * TB), jnp.float32),
        ],
        compiler_params=pltpu.CompilerParams(vmem_limit_bytes=40 * 2**20),
        cost_estimate=pl.CostEstimate(
            flops=8 * rows * heads * slots * HD, bytes_accessed=4 * 2**20,
            transcendentals=rows * heads * slots),
    )(meta, q, k, vt)


def part_kernel(k_ref, v_ref, *refs):
    reqs = (len(refs) - 1) // 2
    scratch = refs[-1]
    n = k_ref.shape[0] // reqs
    scratch[0] = k_ref[...].astype(jnp.float32)
    scratch[1] = v_ref[...].astype(jnp.float32)
    for r in range(reqs):
        refs[r][...] = scratch[0, pl.ds(r, n, stride=reqs), :].astype(jnp.bfloat16)
        refs[reqs + r][...] = scratch[1, pl.ds(r, n, stride=reqs), :].T.astype(jnp.bfloat16)


def part_caches(keys, values):
    slots, reqs, _ = keys.shape
    n = 512
    flat = pl.BlockSpec((n * reqs, HD), lambda i: (i, 0))
    shape = jax.ShapeDtypeStruct((slots, HD), jnp.bfloat16)
    turned = jax.ShapeDtypeStruct((HD, slots), jnp.bfloat16)
    outs = pl.pallas_call(
        part_kernel,
        grid=(slots // n,),
        out_shape=[shape] * reqs + [turned] * reqs,
        in_specs=[flat, flat],
        out_specs=[pl.BlockSpec((n, HD), lambda i: (i, 0))] * reqs
        + [pl.BlockSpec((HD, n), lambda i: (0, i))] * reqs,
        scratch_shapes=[pltpu.VMEM((2, n * reqs, HD), jnp.float32)],
        compiler_params=pltpu.CompilerParams(vmem_limit_bytes=16 * 2**20),
        cost_estimate=pl.CostEstimate(
            flops=0, bytes_accessed=8 * keys.size, transcendentals=0),
    )(keys.reshape(slots * reqs, HD), values.reshape(slots * reqs, HD))
    return outs[:reqs], outs[reqs:]


def merge_kernel(meta, part_ref, out_ref, *, cycle, heads):
    srcs, rows = part_ref.shape[0], part_ref.shape[1]
    tps = srcs // cycle
    width = heads * HD
    keep = lax.broadcasted_iota(jnp.int32, (rows, HD), 0) + meta[1] < meta[0]
    for t in range(tps):
        logs = []
        for c in range(cycle):
            packed = part_ref[c * tps + t, :, width:].astype(jnp.float32)
            logs.append(packed[:, :heads] + packed[:, heads:2 * heads] + packed[:, 2 * heads:3 * heads])
        top = logs[0]
        for ls in logs[1:]:
            top = jnp.maximum(top, ls)
        share = [jnp.exp2(ls - top) for ls in logs]
        total = share[0]
        for s in share[1:]:
            total = total + s
        share = [s / total for s in share]
        for h in range(heads):
            at = slice(h * HD, (h + 1) * HD)
            acc = jnp.zeros((rows, HD), jnp.float32)
            for c in range(cycle):
                acc = acc + share[c][:, h:h + 1] * part_ref[c * tps + t, :, at].astype(jnp.float32)
            out_ref[:, pl.ds(t * width + h * HD, HD)] = jnp.where(keep, acc, 0.0)


def merge(meta, parts, cycle, heads):
    srcs, rows, _ = parts.shape
    tps = srcs // cycle
    return pl.pallas_call(
        lambda *refs: merge_kernel(*refs, cycle=cycle, heads=heads),
        out_shape=jax.ShapeDtypeStruct((rows, tps * heads * HD), jnp.float32),
        in_specs=[pl.BlockSpec(memory_space=pltpu.SMEM), pl.BlockSpec(memory_space=pltpu.VMEM)],
        out_specs=pl.BlockSpec(memory_space=pltpu.VMEM),
        compiler_params=pltpu.CompilerParams(vmem_limit_bytes=40 * 2**20),
        cost_estimate=pl.CostEstimate(
            flops=2 * parts.size, bytes_accessed=2 * parts.size, transcendentals=0),
    )(meta, parts)


def shards(queries, key_cache, value_cache, ctx_len, new_count):
    cycle = lax.axis_size("ctx")
    tps = lax.axis_size("tp")
    here = lax.axis_index("ctx")
    rows, reqs, width = queries.shape
    heads = width // HD
    slots = key_cache.shape[0]
    owners = cycle * tps
    tok_rows = NEWQ // owners
    first_row = (here * tps + lax.axis_index("tp")) * tok_rows
    outs = []
    keys, turned = part_caches(key_cache, value_cache)
    for r in range(reqs):
        q = jnp.broadcast_to(queries[None, :, r], (cycle, rows, width))
        q = lax.all_to_all(q, "ctx", split_axis=0, concat_axis=0).reshape(NEWQ, width)
        part = attend(jnp.stack([ctx_len[r], new_count[r], here * slots]), q, keys[r], turned[r])
        part = part.reshape(owners, tok_rows, width + HD)
        part = lax.all_to_all(part, ("ctx", "tp"), split_axis=0, concat_axis=0)
        outs.append(merge(jnp.stack([new_count[r], first_row]), part, cycle, heads))
    return jnp.stack(outs, axis=1).astype(jnp.bfloat16)


def solution(mesh):
    in_specs = (
        P("ctx", "req", "tp"),
        P("ctx", "req", "tp"),
        P("ctx", "req", "tp"),
        P("req"),
        P("req"),
    )
    out_specs = P(("ctx", "tp"), "req", None)
    return jax.shard_map(shards, mesh=mesh, in_specs=in_specs, out_specs=out_specs, check_vma=False)
```

profile of v0, /device:TPU:1, one launch (start us, length us, event | category | flops | bytes accessed | tf_op | source)
XLA Modules:
  0.0 105.4 jit_solution(18141409866866630395)
XLA Ops:
  0.0 1.5 %fusion = (bf16[32,1,2048]{2,1,0:T(2,128)(2,1)S(1)}, bf16[32,1,2048]{2,1,0:T(2,128)(2,1)S(1)}) fusion(bf16[32,2,2048]{2,1,0:T(2,128)(2,1)} %param.5), kind=kLoop, calls=%fused_computation.9 | loop fusion | bytes 524288 | tf_op jit(solution)/shard_map/slice | solution.py:207
  1.5 0.1 copy.14
  1.6 0.0 copy-start.1
  1.6 1.1 %broadcast_in_dim.17 = bf16[8,32,2048]{2,1,0:T(8,128)(2,1)} broadcast(bf16[32,2048]{1,0:T(8,128)(2,1)S(1)} %bitcast.22), dimensions={1,2} | broadcast | bytes 1179648 | tf_op jit(solution)/shard_map/broadcast_in_dim | solution.py:207
  2.7 0.0 copy-start
  2.7 8.6 %all-to-all-start.2 = ((bf16[8,32,2048]{2,1,0:T(8,128)(2,1)}), bf16[8,32,2048]{2,1,0:T(8,128)(2,1)}, u32[]{:S(2)}, u32[]{:S(2)}) async-start(bf16[8,32,2048]{2,1,0:T(8,128)(2,1)} %broadcast_in_dim.17), calls=%async_computation.2 | async-start | bytes 2097152 | tf_op jit(solution)/shard_map/all_to_all | solution.py:208
  11.3 0.1 copy.15
  11.4 0.0 copy-done.1
  11.4 0.0 copy-done
  11.4 0.0 copy-start.10
  11.4 0.0 copy-start.11
  11.4 1.5 %shard_map.55 = (bf16[3072,128]{1,0:T(8,128)(2,1)S(1)}, bf16[3072,128]{1,0:T(8,128)(2,1)S(1)}, bf16[128,3072]{1,0:T(8,128)(2,1)S(1)}, bf16[128,3072]{1,0:T(8,128)(2,1)S(1)}) custom-call(bf16[6144,128]{1,0:T(8,128)(2,1)S(1)} %bitcast.18, bf16[6144,128]{1,0:T(8,128)(2,1)S(1)} %bitcast.19), custom_call_target="tpu_custom_call" | custom-call | bytes 6291456 | tf_op jit(solution)/shard_map/pallas_call | solution.py:139
  13.0 0.0 copy-start.2
  13.0 0.9 copy-done.2
  13.9 0.0 copy-start.4
  13.9 0.9 copy-done.4
  14.8 0.0 copy-start.6
  14.8 0.9 copy-done.6
  15.7 0.0 copy-start.8
  15.7 0.9 copy-done.8
  16.6 0.0 copy-done.10
  16.6 0.0 copy-done.11
  16.6 0.7 fusion.1
  17.2 0.6 pad_add_fusion.1.refs_0_
  17.9 0.6 pad_add_fusion.refs_0_
  18.5 1.3 %add_add_fusion.1.meta = s32[3]{0:T(128)S(1)} fusion(s32[1]{0:T(128)} %get-tuple-element.19, s32[1]{0:T(128)} %get-tuple-element.16, s32[1]{0:T(128)} %bitcast.1), kind=kLoop, calls=%fused_computation.8 | loop fusion | flops 6 | bytes 24 | tf_op jit(solution)/shard_map/stack | solution.py:209
  19.9 1.3 %add_add_fusion.meta = s32[3]{0:T(128)S(1)} fusion(s32[1]{0:T(128)} %get-tuple-element.20, s32[1]{0:T(128)} %get-tuple-element.15, s32[1]{0:T(128)} %bitcast.1), kind=kLoop, calls=%fused_computation.6 | loop fusion | flops 6 | bytes 24 | tf_op jit(solution)/shard_map/stack | solution.py:209
  21.1 4.4 %all-to-all-done.2 = bf16[8,32,2048]{2,1,0:T(8,128)(2,1)} async-done(((bf16[8,32,2048]{2,1,0:T(8,128)(2,1)}), bf16[8,32,2048]{2,1,0:T(8,128)(2,1)}, u32[]{:S(2)}, u32[]{:S(2)}) %all-to-all-start.2) | async-done | bytes 1048608 | tf_op jit(solution)/shard_map/all_to_all | solution.py:208
  25.6 1.1 %broadcast_in_dim.15 = bf16[8,32,2048]{2,1,0:T(8,128)(2,1)} broadcast(bf16[32,2048]{1,0:T(8,128)(2,1)S(1)} %bitcast.21), dimensions={1,2} | broadcast | bytes 1179648 | tf_op jit(solution)/shard_map/broadcast_in_dim | solution.py:207
  26.7 0.0 copy-start.7
  26.7 0.0 copy-start.9
  26.7 6.1 %all-to-all-start = ((bf16[8,32,2048]{2,1,0:T(8,128)(2,1)}), bf16[8,32,2048]{2,1,0:T(8,128)(2,1)S(1)}, u32[]{:S(2)}, u32[]{:S(2)}) async-start(bf16[8,32,2048]{2,1,0:T(8,128)(2,1)} %broadcast_in_dim.15), calls=%async_computation | async-start | bytes 2097152 | tf_op jit(solution)/shard_map/all_to_all | solution.py:208
  32.8 0.0 copy-done.7
  32.8 0.0 copy-done.9
  32.8 13.0 %shard_map.58 = bf16[256,2176]{1,0:T(8,128)(2,1)} custom-call(s32[3]{0:T(128)S(1)} %add_add_fusion.1.meta, bf16[256,2048]{1,0:T(8,128)(2,1)} %bitcast.9.q_ref, bf16[3072,128]{1,0:T(8,128)(2,1)S(1)} %copy-done.7, bf16[128,3072]{1,0:T(8,128)(2,1)S(1)} %copy-done.9), custom_call_target="tpu_custom_call" | custom-call | flops 12884901888 | bytes 4194304 | tf_op jit(solution)/shard_map/pallas_call | solution.py:106
  45.8 1.4 %all-to-all-done = bf16[8,32,2048]{2,1,0:T(8,128)(2,1)S(1)} async-done(((bf16[8,32,2048]{2,1,0:T(8,128)(2,1)}), bf16[8,32,2048]{2,1,0:T(8,128)(2,1)S(1)}, u32[]{:S(2)}, u32[]{:S(2)}) %all-to-all-start) | async-done | bytes 1048608 | tf_op jit(solution)/shard_map/all_to_all | solution.py:208
  47.2 0.0 copy-start.3
  47.2 8.7 %all-to-all-start.3 = ((bf16[32,8,2176]{2,1,0:T(8,128)(2,1)}), bf16[32,8,2176]{2,1,0:T(8,128)(2,1)S(1)}, u32[]{:S(2)}, u32[]{:S(2)}) async-start(bf16[32,8,2176]{2,1,0:T(8,128)(2,1)} %bitcast.10), calls=%async_computation.3 | async-start | bytes 2228224 | tf_op jit(solution)/shard_map/all_to_all | solution.py:211
  55.9 0.0 copy-done.3
  55.9 0.0 copy-start.5
  55.9 1.1 %copy-done.5 = bf16[128,3072]{1,0:T(8,128)(2,1)S(1)} copy-done((bf16[128,3072]{1,0:T(8,128)(2,1)S(1)}, bf16[128,3072]{1,0:T(8,128)(2,1)}, u32[]{:S(2)}) %copy-start.5) | copy-done | bytes 786456
  57.0 18.0 %shard_map.56 = bf16[256,2176]{1,0:T(8,128)(2,1)} custom-call(s32[3]{0:T(128)S(1)} %add_add_fusion.meta, bf16[256,2048]{1,0:T(8,128)(2,1)S(1)} %bitcast.20, bf16[3072,128]{1,0:T(8,128)(2,1)S(1)} %copy-done.3, bf16[128,3072]{1,0:T(8,128)(2,1)S(1)} %copy-done.5), custom_call_target="tpu_custom_call" | custom-call | flops 12884901888 | bytes 4194304 | tf_op jit(solution)/shard_map/pallas_call | solution.py:106
  75.0 0.0 all-to-all-done.3.refs_1_
  75.0 9.3 %all-to-all-start.1 = ((bf16[32,8,2176]{2,1,0:T(8,128)(2,1)}), bf16[32,8,2176]{2,1,0:T(8,128)(2,1)S(1)}, u32[]{:S(2)}, u32[]{:S(2)}) async-start(bf16[32,8,2176]{2,1,0:T(8,128)(2,1)} %bitcast.6), calls=%async_computation.1 | async-start | bytes 2228224 | tf_op jit(solution)/shard_map/all_to_all | solution.py:211
  84.3 1.9 %shard_map.59 = f32[8,8192]{1,0:T(8,128)S(1)} custom-call(s32[2]{0:T(128)S(1)} %pad_add_fusion.1.refs_0_, bf16[32,8,2176]{2,1,0:T(8,128)(2,1)S(1)} %all-to-all-done.3.refs_1_), custom_call_target="tpu_custom_call" | custom-call | flops 1114112 | bytes 1114112 | tf_op jit(solution)/shard_map/pallas_call | solution.py:183
  86.2 16.2 %all-to-all-done.1.refs_1_ = bf16[32,8,2176]{2,1,0:T(8,128)(2,1)S(1)} async-done(((bf16[32,8,2176]{2,1,0:T(8,128)(2,1)}), bf16[32,8,2176]{2,1,0:T(8,128)(2,1)S(1)}, u32[]{:S(2)}, u32[]{:S(2)}) %all-to-all-start.1) | async-done | bytes 1114144 | tf_op jit(solution)/shard_map/all_to_all | solution.py:211
  102.5 1.9 %shard_map.57 = f32[8,8192]{1,0:T(8,128)S(1)} custom-call(s32[2]{0:T(128)S(1)} %pad_add_fusion.refs_0_, bf16[32,8,2176]{2,1,0:T(8,128)(2,1)S(1)} %all-to-all-done.1.refs_1_), custom_call_target="tpu_custom_call" | custom-call | flops 1114112 | bytes 1114112 | tf_op jit(solution)/shard_map/pallas_call | solution.py:183
  104.4 1.0 copy.9
  (3 shorter events, 0.1 us)
Async XLA Ops:
  1.6 9.8 %copy-start.1 = (bf16[3072,2,128]{2,1,0:T(2,128)(2,1)S(1)}, bf16[3072,2,128]{2,1,0:T(2,128)(2,1)}, u32[]{:S(2)}) copy-start(bf16[3072,2,128]{2,1,0:T(2,128)(2,1)} %param.7) | copy-start | bytes 4718596
  2.7 8.7 %copy-start = (bf16[3072,2,128]{2,1,0:T(2,128)(2,1)S(1)}, bf16[3072,2,128]{2,1,0:T(2,128)(2,1)}, u32[]{:S(2)}) copy-start(bf16[3072,2,128]{2,1,0:T(2,128)(2,1)} %param.6) | copy-start | bytes 4718596
  2.7 22.9 %all-to-all-start.2 = ((bf16[8,32,2048]{2,1,0:T(8,128)(2,1)}), bf16[8,32,2048]{2,1,0:T(8,128)(2,1)}, u32[]{:S(2)}, u32[]{:S(2)}) async-start(bf16[8,32,2048]{2,1,0:T(8,128)(2,1)} %broadcast_in_dim.17), calls=%async_computation.2 | async-start | bytes 2097152 | tf_op jit(solution)/shard_map/all_to_all | solution.py:208
  11.4 5.2 %copy-start.10 = (s32[2]{0:T(128)S(1)}, s32[2]{0:T(128)}, u32[]{:S(2)}) copy-start(s32[2]{0:T(128)} %param.8) | copy-start | bytes 28
  11.4 5.1 %copy-start.11 = (s32[2]{0:T(128)S(1)}, s32[2]{0:T(128)}, u32[]{:S(2)}) copy-start(s32[2]{0:T(128)} %param.9) | copy-start | bytes 28
  13.0 0.9 copy-start.2
  13.9 0.9 copy-start.4
  14.8 0.9 copy-start.6
  15.7 0.9 copy-start.8
  26.7 6.1 %copy-start.7 = (bf16[3072,128]{1,0:T(8,128)(2,1)S(1)}, bf16[3072,128]{1,0:T(8,128)(2,1)}, u32[]{:S(2)}) copy-start(bf16[3072,128]{1,0:T(8,128)(2,1)} %copy-done.6) | copy-start | bytes 2359300
  26.7 6.1 %copy-start.9 = (bf16[128,3072]{1,0:T(8,128)(2,1)S(1)}, bf16[128,3072]{1,0:T(8,128)(2,1)}, u32[]{:S(2)}) copy-start(bf16[128,3072]{1,0:T(8,128)(2,1)} %copy-done.8) | copy-start | bytes 2359300
  26.7 20.5 %all-to-all-start = ((bf16[8,32,2048]{2,1,0:T(8,128)(2,1)}), bf16[8,32,2048]{2,1,0:T(8,128)(2,1)S(1)}, u32[]{:S(2)}, u32[]{:S(2)}) async-start(bf16[8,32,2048]{2,1,0:T(8,128)(2,1)} %broadcast_in_dim.15), calls=%async_computation | async-start | bytes 2097152 | tf_op jit(solution)/shard_map/all_to_all | solution.py:208
  47.2 8.7 %copy-start.3 = (bf16[3072,128]{1,0:T(8,128)(2,1)S(1)}, bf16[3072,128]{1,0:T(8,128)(2,1)}, u32[]{:S(2)}) copy-start(bf16[3072,128]{1,0:T(8,128)(2,1)} %copy-done.2) | copy-start | bytes 2359300
  47.2 27.8 %all-to-all-start.3 = ((bf16[32,8,2176]{2,1,0:T(8,128)(2,1)}), bf16[32,8,2176]{2,1,0:T(8,128)(2,1)S(1)}, u32[]{:S(2)}, u32[]{:S(2)}) async-start(bf16[32,8,2176]{2,1,0:T(8,128)(2,1)} %bitcast.10), calls=%async_computation.3 | async-start | bytes 2228224 | tf_op jit(solution)/shard_map/all_to_all | solution.py:211
  55.9 1.1 %copy-start.5 = (bf16[128,3072]{1,0:T(8,128)(2,1)S(1)}, bf16[128,3072]{1,0:T(8,128)(2,1)}, u32[]{:S(2)}) copy-start(bf16[128,3072]{1,0:T(8,128)(2,1)} %copy-done.4) | copy-start | bytes 2359300
  75.0 27.4 %all-to-all-start.1 = ((bf16[32,8,2176]{2,1,0:T(8,128)(2,1)}), bf16[32,8,2176]{2,1,0:T(8,128)(2,1)S(1)}, u32[]{:S(2)}, u32[]{:S(2)}) async-start(bf16[32,8,2176]{2,1,0:T(8,128)(2,1)} %bitcast.6), calls=%async_computation.1 | async-start | bytes 2228224 | tf_op jit(solution)/shard_map/all_to_all | solution.py:211
where the time goes:
time: 106 us; the launch traced here: 105 us
  Pallas kernels  36.3 us (34%)
  starting transfers between devices  32.7 us (31%)
  waiting for transfers between devices  22 us (21%)
  local copies, waits for them, and re-layouts  10.2 us (10%)
  other arithmetic  3.97 us (4%)
    pallas_call x2, Pallas kernels, attend(): pl.pallas_call(attend_kernel, out_shape=jax.ShapeDtypeStruct((rows, width...  30.9 us
    all_to_all x2, starting transfers between devices, shards(): part = lax.all_to_all(part, ('ctx', 'tp'), split_axis=0, concat_axis=0)  18 us
    all_to_all x2, waiting for transfers between devices, shards(): part = lax.all_to_all(part, ('ctx', 'tp'), split_axis=0, concat_axis=0)  16.2 us
    all_to_all x2, starting transfers between devices, shards(): lax.all_to_all(q, 'ctx', split_axis=0, concat_axis=0).reshape(NEWQ, width)  14.7 us
    all_to_all x2, waiting for transfers between devices, shards(): lax.all_to_all(q, 'ctx', split_axis=0, concat_axis=0).reshape(NEWQ, width)  5.83 us
    unnamed x26, local copies, waits for them, and re-layouts  4.91 us
    pallas_call x2, Pallas kernels, merge(): pl.pallas_call(lambda *refs: merge_kernel(*refs, cycle=cycle, heads=heads...  3.87 us
    another operation x2, other arithmetic, shards(): jnp.stack([ctx_len[r], new_count[r], here * slots])  2.63 us
  transfers between devices with their start and end apart: 4, of which 3 were waited for; matrix products, arithmetic and copies ran while one was open for 4% of the time, Pallas kernels for 33%

commit v1 on v0

--- a/solution.py
+++ b/solution.py
@@ -1,3 +1,4 @@
+import functools
 import math
 
 import jax
@@ -26,15 +27,25 @@
     return packed.astype(jnp.bfloat16)
 
 
-def attend_kernel(meta, q_ref, k_ref, vt_ref, o_ref, s, mx):
+def attend_kernel(req, meta, *refs):
+    *q_refs, k_ref, vt_ref, o_ref, s, mx, q_all = refs
     slots = k_ref.shape[0]
-    width = q_ref.shape[1]
+    width = k_ref.shape[1] * ((o_ref.shape[1] - HD) // HD)
     heads = width // HD
     lanes = heads * TB
-    ctx_len, new_count, base = meta[0], meta[1], meta[2]
+    reqs = (meta.shape[0] - 4) // 2
+    ctx_len, new_count, base = meta[req], meta[reqs + req], meta[2 * reqs]
     edge = ctx_len - base + 1
     some = edge + NEWQ - 1 > 0
     tiles = jnp.where(some, (new_count + TB - 1) // TB, 0)
+    q_ref = q_refs[0]
+    if len(q_refs) > 1:
+        ring = len(q_refs)
+        q_ref = q_all
+        for n, pair in enumerate(q_refs):
+            for m in range(2):
+                block = (meta[2 * reqs + 1] + m) % 2 * ring + (meta[2 * reqs + 2] - n + ring) % ring
+                q_all[pl.ds(pl.multiple_of(block * TB, TB), TB), :] = pair[m * TB:(m + 1) * TB, :]
     of_head = lax.broadcasted_iota(jnp.int32, (TB, HD), 1) % heads
     token = lax.broadcasted_iota(jnp.int32, (1, lanes), 1) % TB
     key = lax.broadcasted_iota(jnp.int32, (KC, lanes), 0)
@@ -99,24 +110,25 @@
             run(span, clear)
 
 
-def attend(meta, q, k, vt):
-    rows, width = q.shape
+def attend(req, meta, qs, k, vt):
+    rows, width = NEWQ, qs[0].shape[1]
     slots = k.shape[0]
     heads = width // HD
     return pl.pallas_call(
-        attend_kernel,
+        functools.partial(attend_kernel, req),
         out_shape=jax.ShapeDtypeStruct((rows, width + HD), jnp.bfloat16),
-        in_specs=[SMEM, VMEM, VMEM, VMEM],
+        in_specs=[SMEM] + [VMEM] * (len(qs) + 2),
         out_specs=VMEM,
         scratch_shapes=[
             pltpu.VMEM((slots, heads * TB), jnp.float32),
             pltpu.VMEM((8, heads * TB), jnp.float32),
+            pltpu.VMEM((rows if len(qs) > 1 else TB, width), jnp.bfloat16),
         ],
         compiler_params=pltpu.CompilerParams(vmem_limit_bytes=40 * 2**20),
         cost_estimate=pl.CostEstimate(
             flops=8 * rows * heads * slots * HD, bytes_accessed=4 * 2**20,
             transcendentals=rows * heads * slots),
-    )(meta, q, k, vt)
+    )(meta, *qs, k, vt)
 
 
 def part_kernel(k_ref, v_ref, *refs):
@@ -151,11 +163,11 @@
     return outs[:reqs], outs[reqs:]
 
 
-def merge_kernel(meta, part_ref, out_ref, *, cycle, heads):
+def merge_kernel(req, meta, part_ref, out_ref, *, cycle, heads):
     srcs, rows = part_ref.shape[0], part_ref.shape[1]
     tps = srcs // cycle
     width = heads * HD
-    keep = lax.broadcasted_iota(jnp.int32, (rows, HD), 0) + meta[1] < meta[0]
+    keep = lax.broadcasted_iota(jnp.int32, (rows, HD), 0) + meta[meta.shape[0] - 1] < meta[(meta.shape[0] - 4) // 2 + req]
     for t in range(tps):
         logs = []
         for c in range(cycle):
@@ -177,11 +189,11 @@
             out_ref[:, pl.ds(t * width + h * HD, HD)] = jnp.where(keep, acc, 0.0)
 
 
-def merge(meta, parts, cycle, heads):
+def merge(req, meta, parts, cycle, heads):
     srcs, rows, _ = parts.shape
     tps = srcs // cycle
     return pl.pallas_call(
-        lambda *refs: merge_kernel(*refs, cycle=cycle, heads=heads),
+        functools.partial(merge_kernel, req, cycle=cycle, heads=heads),
         out_shape=jax.ShapeDtypeStruct((rows, tps * heads * HD), jnp.float32),
         in_specs=[pl.BlockSpec(memory_space=pltpu.SMEM), pl.BlockSpec(memory_space=pltpu.VMEM)],
         out_specs=pl.BlockSpec(memory_space=pltpu.VMEM),
@@ -189,6 +201,15 @@
         cost_estimate=pl.CostEstimate(
             flops=2 * parts.size, bytes_accessed=2 * parts.size, transcendentals=0),
     )(meta, parts)
+
+
+def shifted(block, across, along):
+    size = lax.axis_size("ctx")
+    ring = size // 2
+    route = [
+        (i, (i // ring + across) % 2 * ring + (i % ring + along) % ring) for i in range(size)
+    ]
+    return lax.ppermute(block, "ctx", route)
 
 
 def shards(queries, key_cache, value_cache, ctx_len, new_count):
@@ -201,15 +222,20 @@
     owners = cycle * tps
     tok_rows = NEWQ // owners
     first_row = (here * tps + lax.axis_index("tp")) * tok_rows
+    ring = cycle // 2
+    places = jnp.stack([here * slots, here // ring, here % ring, first_row])
+    meta = jnp.concatenate([ctx_len, new_count, places])
+    split = queries.transpose(1, 0, 2)
+    caches = part_caches(key_cache, value_cache)
+    other, meta, (keys, turned) = lax.optimization_barrier((shifted(split, 1, 0), meta, caches))
+    pairs = jnp.concatenate([split, other], axis=1)
     outs = []
-    keys, turned = part_caches(key_cache, value_cache)
     for r in range(reqs):
-        q = jnp.broadcast_to(queries[None, :, r], (cycle, rows, width))
-        q = lax.all_to_all(q, "ctx", split_axis=0, concat_axis=0).reshape(NEWQ, width)
-        part = attend(jnp.stack([ctx_len[r], new_count[r], here * slots]), q, keys[r], turned[r])
+        qs = [pairs[r]] + [shifted(pairs[r], 0, n) for n in range(1, ring)]
+        part = attend(r, meta, qs, keys[r], turned[r])
         part = part.reshape(owners, tok_rows, width + HD)
         part = lax.all_to_all(part, ("ctx", "tp"), split_axis=0, concat_axis=0)
-        outs.append(merge(jnp.stack([new_count[r], first_row]), part, cycle, heads))
+        outs.append(merge(r, meta, part, cycle, heads))
     return jnp.stack(outs, axis=1).astype(jnp.bfloat16)
 
 

time: 106 us -> 104 us (0.981)
  the two profiles are of different devices: /device:TPU:1 before, /device:TPU:0 now
where the time goes in v1:
time: 104 us; the launch traced here: 102 us
  Pallas kernels  41.3 us (40%)
  starting transfers between devices  26.7 us (26%)
  waiting for transfers between devices  26.5 us (25%)
  local copies, waits for them, and re-layouts  6.93 us (7%)
    pallas_call x2, Pallas kernels, attend(): pl.pallas_call(functools.partial(attend_kernel, req), out_shape=jax.Shape...  35.9 us
    all_to_all x2, starting transfers between devices, shards(): part = lax.all_to_all(part, ('ctx', 'tp'), split_axis=0, concat_axis=0)  13.6 us
    all_to_all x2, waiting for transfers between devices, shards(): part = lax.all_to_all(part, ('ctx', 'tp'), split_axis=0, concat_axis=0)  13.5 us
    ppermute x7, starting transfers between devices, shifted(): return lax.ppermute(block, 'ctx', route)  13.1 us
    ppermute x7, waiting for transfers between devices, shifted(): return lax.ppermute(block, 'ctx', route)  13 us
    unnamed x13, local copies, waits for them, and re-layouts  5.87 us
    pallas_call x2, Pallas kernels, merge(): pl.pallas_call(functools.partial(merge_kernel, req, cycle=cycle, heads=he...  3.84 us
  transfers between devices with their start and end apart: 9, of which 5 were waited for; matrix products, arithmetic and copies ran while one was open for 0% of the time, Pallas kernels for 39%

profile of v1, /device:TPU:0, one launch (start us, length us, event | category | flops | bytes accessed | tf_op | source)
XLA Modules:
  0.0 101.6 jit_solution(11917443840963566706)
XLA Ops:
  0.0 1.0 %copy.9 = bf16[32,2,2048]{2,0,1:T(8,128)(2,1)S(1)} copy(bf16[32,2,2048]{2,1,0:T(2,128)(2,1)} %param.5) | data formatting | bytes 524288 | tf_op args[0]
  1.0 3.4 %collective-permute-start = (bf16[2,32,2048]{2,1,0:T(8,128)(2,1)S(1)}, bf16[2,32,2048]{2,1,0:T(8,128)(2,1)S(1)}, u32[]{:S(2)}, u32[]{:S(2)}) collective-permute-start(bf16[2,32,2048]{2,1,0:T(8,128)(2,1)S(1)} %bitcast.21), channel_id=1, source_target_pairs={{0,64},{16,80},{32,96},{48,112},{64,0},{80,16},{96,32},{112,48},{1... | collective-permute-start | bytes 786440 | tf_op jit(solution)/shard_map/ppermute | solution.py:212
  4.4 0.0 copy-start
  4.4 1.4 %copy-done = bf16[3072,2,128]{2,1,0:T(2,128)(2,1)S(1)} copy-done((bf16[3072,2,128]{2,1,0:T(2,128)(2,1)S(1)}, bf16[3072,2,128]{2,1,0:T(2,128)(2,1)}, u32[]{:S(2)}) %copy-start) | copy-done | bytes 1572888
  5.8 0.0 copy-start.1
  5.8 1.4 %copy-done.1 = bf16[3072,2,128]{2,1,0:T(2,128)(2,1)S(1)} copy-done((bf16[3072,2,128]{2,1,0:T(2,128)(2,1)S(1)}, bf16[3072,2,128]{2,1,0:T(2,128)(2,1)}, u32[]{:S(2)}) %copy-start.1) | copy-done | bytes 1572888
  7.2 0.0 copy-start.4
  7.2 0.0 copy-start.5
  7.2 1.5 %shard_map.55 = (bf16[3072,128]{1,0:T(8,128)(2,1)S(1)}, bf16[3072,128]{1,0:T(8,128)(2,1)S(1)}, bf16[128,3072]{1,0:T(8,128)(2,1)S(1)}, bf16[128,3072]{1,0:T(8,128)(2,1)S(1)}) custom-call(bf16[6144,128]{1,0:T(8,128)(2,1)S(1)} %bitcast.19, bf16[6144,128]{1,0:T(8,128)(2,1)S(1)} %bitcast.20), custom_call_target="tpu_custom_call" | custom-call | bytes 6291456 | tf_op jit(solution)/shard_map/pallas_call | solution.py:151
  8.7 0.0 copy-start.2
  8.7 0.9 copy-done.2
  9.6 0.0 copy-done.4
  9.6 0.0 copy-done.5
  9.6 0.1 concatenate.6.meta
  9.7 1.0 collective-permute-done
  10.7 4.2 %collective-permute-start.3 = (bf16[64,2048]{1,0:T(8,128)(2,1)S(1)}, bf16[64,2048]{1,0:T(8,128)(2,1)S(1)}, u32[]{:S(2)}, u32[]{:S(2)}) collective-permute-start(bf16[64,2048]{1,0:T(8,128)(2,1)S(1)} %get-tuple-element.25.refs_0_), channel_id=1, source_target_pairs={{0,48},{16,0},{32,16},{48,32},{64,112},{80,64},{96,80},{112,96},{1... | collective-permute-start | bytes 786440 | tf_op jit(solution)/shard_map/ppermute | solution.py:212
  14.9 0.0 collective-permute-start.2
  14.9 1.3 %collective-permute-start.1 = (bf16[64,2048]{1,0:T(8,128)(2,1)S(1)}, bf16[64,2048]{1,0:T(8,128)(2,1)S(1)}, u32[]{:S(2)}, u32[]{:S(2)}) collective-permute-start(bf16[64,2048]{1,0:T(8,128)(2,1)S(1)} %get-tuple-element.25.refs_0_), channel_id=1, source_target_pairs={{0,16},{16,32},{32,48},{48,0},{64,80},{80,96},{96,112},{112,64},{1... | collective-permute-start | bytes 786440 | tf_op jit(solution)/shard_map/ppermute | solution.py:212
  16.2 2.0 %collective-permute-start.6 = (bf16[64,2048]{1,0:T(8,128)(2,1)S(1)}, bf16[64,2048]{1,0:T(8,128)(2,1)S(1)}, u32[]{:S(2)}, u32[]{:S(2)}) collective-permute-start(bf16[64,2048]{1,0:T(8,128)(2,1)S(1)} %get-tuple-element.26.refs_0_), channel_id=1, source_target_pairs={{0,48},{16,0},{32,16},{48,32},{64,112},{80,64},{96,80},{112,96},{1... | collective-permute-start | bytes 786440 | tf_op jit(solution)/shard_map/ppermute | solution.py:212
  18.1 2.3 %collective-permute-start.5 = (bf16[64,2048]{1,0:T(8,128)(2,1)S(1)}, bf16[64,2048]{1,0:T(8,128)(2,1)S(1)}, u32[]{:S(2)}, u32[]{:S(2)}) collective-permute-start(bf16[64,2048]{1,0:T(8,128)(2,1)S(1)} %get-tuple-element.26.refs_0_), channel_id=1, source_target_pairs={{0,32},{16,48},{32,0},{48,16},{64,96},{80,112},{96,64},{112,80},{1... | collective-permute-start | bytes 786440 | tf_op jit(solution)/shard_map/ppermute | solution.py:212
  20.5 6.4 %collective-permute-done.3.refs_3_ = bf16[64,2048]{1,0:T(8,128)(2,1)S(1)} collective-permute-done((bf16[64,2048]{1,0:T(8,128)(2,1)S(1)}, bf16[64,2048]{1,0:T(8,128)(2,1)S(1)}, u32[]{:S(2)}, u32[]{:S(2)}) %collective-permute-start.3) | collective-permute-done | bytes 262176 | tf_op jit(solution)/shard_map/ppermute | solution.py:212
  26.8 0.0 collective-permute-start.4
  26.8 0.0 collective-permute-done.2.refs_2_
  26.8 5.7 %collective-permute-done.1.refs_1_ = bf16[64,2048]{1,0:T(8,128)(2,1)S(1)} collective-permute-done((bf16[64,2048]{1,0:T(8,128)(2,1)S(1)}, bf16[64,2048]{1,0:T(8,128)(2,1)S(1)}, u32[]{:S(2)}, u32[]{:S(2)}) %collective-permute-start.1) | collective-permute-done | bytes 262176 | tf_op jit(solution)/shard_map/ppermute | solution.py:212
  32.5 0.0 copy-start.3
  32.5 1.1 %copy-done.3 = bf16[128,3072]{1,0:T(8,128)(2,1)S(1)} copy-done((bf16[128,3072]{1,0:T(8,128)(2,1)S(1)}, bf16[128,3072]{1,0:T(8,128)(2,1)}, u32[]{:S(2)}) %copy-start.3) | copy-done | bytes 786456
  33.6 17.8 %shard_map.56 = bf16[256,2176]{1,0:T(8,128)(2,1)} custom-call(s32[8]{0:T(128)S(1)} %concatenate.6.meta, bf16[64,2048]{1,0:T(8,128)(2,1)S(1)} %get-tuple-element.25.refs_0_, bf16[64,2048]{1,0:T(8,128)(2,1)S(1)} %collective-permute-done.1.refs_1_, bf16[64,2048]{1,0:T(8,128)(2,1)S(1)} %collective-permute-done.2.refs_2_, ...), custom_call_target="tpu_custom_call" | custom-call | flops 12884901888 | bytes 4194304 | tf_op jit(solution)/shard_map/pallas_call | solution.py:117
  51.4 4.8 %all-to-all-start = ((bf16[32,8,2176]{2,1,0:T(8,128)(2,1)}), bf16[32,8,2176]{2,1,0:T(8,128)(2,1)S(1)}, u32[]{:S(2)}, u32[]{:S(2)}) async-start(bf16[32,8,2176]{2,1,0:T(8,128)(2,1)} %bitcast.8), calls=%async_computation | async-start | bytes 2228224 | tf_op jit(solution)/shard_map/all_to_all | solution.py:237
  56.2 0.0 collective-permute-done.6.refs_3_
  56.2 0.0 collective-permute-done.5.refs_2_
  56.2 0.0 collective-permute-done.4.refs_1_
  56.2 18.2 %shard_map.58 = bf16[256,2176]{1,0:T(8,128)(2,1)} custom-call(s32[8]{0:T(128)S(1)} %concatenate.6.meta, bf16[64,2048]{1,0:T(8,128)(2,1)S(1)} %get-tuple-element.26.refs_0_, bf16[64,2048]{1,0:T(8,128)(2,1)} %collective-permute-done.4.refs_1_, bf16[64,2048]{1,0:T(8,128)(2,1)S(1)} %collective-permute-done.5.refs_2_, ...), custom_call_target="tpu_custom_call" | custom-call | flops 12884901888 | bytes 4194304 | tf_op jit(solution)/shard_map/pallas_call | solution.py:117
  74.4 1.0 all-to-all-done.part_ref
  75.4 8.8 %all-to-all-start.1 = ((bf16[32,8,2176]{2,1,0:T(8,128)(2,1)}), bf16[32,8,2176]{2,1,0:T(8,128)(2,1)S(1)}, u32[]{:S(2)}, u32[]{:S(2)}) async-start(bf16[32,8,2176]{2,1,0:T(8,128)(2,1)} %bitcast.11), calls=%async_computation.1 | async-start | bytes 2228224 | tf_op jit(solution)/shard_map/all_to_all | solution.py:237
  84.2 1.9 %shard_map.57 = f32[8,8192]{1,0:T(8,128)S(1)} custom-call(s32[8]{0:T(128)S(1)} %concatenate.6.meta, bf16[32,8,2176]{2,1,0:T(8,128)(2,1)S(1)} %all-to-all-done.part_ref), custom_call_target="tpu_custom_call" | custom-call | flops 1114112 | bytes 1114112 | tf_op jit(solution)/shard_map/pallas_call | solution.py:195
  86.2 12.5 %all-to-all-done.1.part_ref = bf16[32,8,2176]{2,1,0:T(8,128)(2,1)S(1)} async-done(((bf16[32,8,2176]{2,1,0:T(8,128)(2,1)}), bf16[32,8,2176]{2,1,0:T(8,128)(2,1)S(1)}, u32[]{:S(2)}, u32[]{:S(2)}) %all-to-all-start.1) | async-done | bytes 1114144 | tf_op jit(solution)/shard_map/all_to_all | solution.py:237
  98.6 1.9 %shard_map.59 = f32[8,8192]{1,0:T(8,128)S(1)} custom-call(s32[8]{0:T(128)S(1)} %concatenate.6.meta, bf16[32,8,2176]{2,1,0:T(8,128)(2,1)S(1)} %all-to-all-done.1.part_ref), custom_call_target="tpu_custom_call" | custom-call | flops 1114112 | bytes 1114112 | tf_op jit(solution)/shard_map/pallas_call | solution.py:195
  100.6 1.0 copy.7
  (4 shorter events, 0.1 us)
Async XLA Ops:
  1.0 9.7 %collective-permute-start = (bf16[2,32,2048]{2,1,0:T(8,128)(2,1)S(1)}, bf16[2,32,2048]{2,1,0:T(8,128)(2,1)S(1)}, u32[]{:S(2)}, u32[]{:S(2)}) collective-permute-start(bf16[2,32,2048]{2,1,0:T(8,128)(2,1)S(1)} %bitcast.21), channel_id=1, source_target_pairs={{0,64},{16,80},{32,96},{48,112},{64,0},{80,16},{96,32},{112,48},{1... | collective-permute-start | bytes 786440 | tf_op jit(solution)/shard_map/ppermute | solution.py:212
  4.4 1.4 %copy-start = (bf16[3072,2,128]{2,1,0:T(2,128)(2,1)S(1)}, bf16[3072,2,128]{2,1,0:T(2,128)(2,1)}, u32[]{:S(2)}) copy-start(bf16[3072,2,128]{2,1,0:T(2,128)(2,1)} %param.6) | copy-start | bytes 4718596
  5.8 1.4 %copy-start.1 = (bf16[3072,2,128]{2,1,0:T(2,128)(2,1)S(1)}, bf16[3072,2,128]{2,1,0:T(2,128)(2,1)}, u32[]{:S(2)}) copy-start(bf16[3072,2,128]{2,1,0:T(2,128)(2,1)} %param.7) | copy-start | bytes 4718596
  7.2 2.4 %copy-start.4 = (s32[2]{0:T(128)S(1)}, s32[2]{0:T(128)}, u32[]{:S(2)}) copy-start(s32[2]{0:T(128)} %param.8) | copy-start | bytes 28
  7.2 2.4 %copy-start.5 = (s32[2]{0:T(128)S(1)}, s32[2]{0:T(128)}, u32[]{:S(2)}) copy-start(s32[2]{0:T(128)} %param.9) | copy-start | bytes 28
  8.7 0.9 copy-start.2
  10.7 16.1 %collective-permute-start.3 = (bf16[64,2048]{1,0:T(8,128)(2,1)S(1)}, bf16[64,2048]{1,0:T(8,128)(2,1)S(1)}, u32[]{:S(2)}, u32[]{:S(2)}) collective-permute-start(bf16[64,2048]{1,0:T(8,128)(2,1)S(1)} %get-tuple-element.25.refs_0_), channel_id=1, source_target_pairs={{0,48},{16,0},{32,16},{48,32},{64,112},{80,64},{96,80},{112,96},{1... | collective-permute-start | bytes 786440 | tf_op jit(solution)/shard_map/ppermute | solution.py:212
  14.9 11.9 %collective-permute-start.2 = (bf16[64,2048]{1,0:T(8,128)(2,1)S(1)}, bf16[64,2048]{1,0:T(8,128)(2,1)S(1)}, u32[]{:S(2)}, u32[]{:S(2)}) collective-permute-start(bf16[64,2048]{1,0:T(8,128)(2,1)S(1)} %get-tuple-element.25.refs_0_), channel_id=1, source_target_pairs={{0,32},{16,48},{32,0},{48,16},{64,96},{80,112},{96,64},{112,80},{1... | collective-permute-start | bytes 786440 | tf_op jit(solution)/shard_map/ppermute | solution.py:212
  14.9 17.6 %collective-permute-start.1 = (bf16[64,2048]{1,0:T(8,128)(2,1)S(1)}, bf16[64,2048]{1,0:T(8,128)(2,1)S(1)}, u32[]{:S(2)}, u32[]{:S(2)}) collective-permute-start(bf16[64,2048]{1,0:T(8,128)(2,1)S(1)} %get-tuple-element.25.refs_0_), channel_id=1, source_target_pairs={{0,16},{16,32},{32,48},{48,0},{64,80},{80,96},{96,112},{112,64},{1... | collective-permute-start | bytes 786440 | tf_op jit(solution)/shard_map/ppermute | solution.py:212
  16.2 40.0 %collective-permute-start.6 = (bf16[64,2048]{1,0:T(8,128)(2,1)S(1)}, bf16[64,2048]{1,0:T(8,128)(2,1)S(1)}, u32[]{:S(2)}, u32[]{:S(2)}) collective-permute-start(bf16[64,2048]{1,0:T(8,128)(2,1)S(1)} %get-tuple-element.26.refs_0_), channel_id=1, source_target_pairs={{0,48},{16,0},{32,16},{48,32},{64,112},{80,64},{96,80},{112,96},{1... | collective-permute-start | bytes 786440 | tf_op jit(solution)/shard_map/ppermute | solution.py:212
  18.1 38.1 %collective-permute-start.5 = (bf16[64,2048]{1,0:T(8,128)(2,1)S(1)}, bf16[64,2048]{1,0:T(8,128)(2,1)S(1)}, u32[]{:S(2)}, u32[]{:S(2)}) collective-permute-start(bf16[64,2048]{1,0:T(8,128)(2,1)S(1)} %get-tuple-element.26.refs_0_), channel_id=1, source_target_pairs={{0,32},{16,48},{32,0},{48,16},{64,96},{80,112},{96,64},{112,80},{1... | collective-permute-start | bytes 786440 | tf_op jit(solution)/shard_map/ppermute | solution.py:212
  26.8 29.4 %collective-permute-start.4 = (bf16[64,2048]{1,0:T(8,128)(2,1)S(1)}, bf16[64,2048]{1,0:T(8,128)(2,1)}, u32[]{:S(2)}, u32[]{:S(2)}) collective-permute-start(bf16[64,2048]{1,0:T(8,128)(2,1)S(1)} %get-tuple-element.26.refs_0_), channel_id=1, source_target_pairs={{0,16},{16,32},{32,48},{48,0},{64,80},{80,96},{96,112},{112,64},{1... | collective-permute-start | bytes 786440 | tf_op jit(solution)/shard_map/ppermute | solution.py:212
  32.5 1.1 %copy-start.3 = (bf16[128,3072]{1,0:T(8,128)(2,1)S(1)}, bf16[128,3072]{1,0:T(8,128)(2,1)}, u32[]{:S(2)}) copy-start(bf16[128,3072]{1,0:T(8,128)(2,1)} %copy-done.2) | copy-start | bytes 2359300
  51.4 24.0 %all-to-all-start = ((bf16[32,8,2176]{2,1,0:T(8,128)(2,1)}), bf16[32,8,2176]{2,1,0:T(8,128)(2,1)S(1)}, u32[]{:S(2)}, u32[]{:S(2)}) async-start(bf16[32,8,2176]{2,1,0:T(8,128)(2,1)} %bitcast.8), calls=%async_computation | async-start | bytes 2228224 | tf_op jit(solution)/shard_map/all_to_all | solution.py:237
  75.4 23.3 %all-to-all-start.1 = ((bf16[32,8,2176]{2,1,0:T(8,128)(2,1)}), bf16[32,8,2176]{2,1,0:T(8,128)(2,1)S(1)}, u32[]{:S(2)}, u32[]{:S(2)}) async-start(bf16[32,8,2176]{2,1,0:T(8,128)(2,1)} %bitcast.11), calls=%async_computation.1 | async-start | bytes 2228224 | tf_op jit(solution)/shard_map/all_to_all | solution.py:237

commit v2 on v1

--- a/solution.py
+++ b/solution.py
@@ -27,46 +27,57 @@
     return packed.astype(jnp.bfloat16)
 
 
-def attend_kernel(req, meta, *refs):
-    *q_refs, k_ref, vt_ref, o_ref, s, mx, q_all = refs
-    slots = k_ref.shape[0]
-    width = k_ref.shape[1] * ((o_ref.shape[1] - HD) // HD)
+def sweep(req, place, lead, meta, q_ref, k_ref, vt_ref, o_ref, s, mx, order):
+    slots = k_ref.shape[1]
+    width = q_ref.shape[2]
     heads = width // HD
     lanes = heads * TB
+    count = q_ref.shape[1] // TB
     reqs = (meta.shape[0] - 4) // 2
+    ring = NEWQ // TB // 2
     ctx_len, new_count, base = meta[req], meta[reqs + req], meta[2 * reqs]
     edge = ctx_len - base + 1
     some = edge + NEWQ - 1 > 0
-    tiles = jnp.where(some, (new_count + TB - 1) // TB, 0)
-    q_ref = q_refs[0]
-    if len(q_refs) > 1:
-        ring = len(q_refs)
-        q_ref = q_all
-        for n, pair in enumerate(q_refs):
-            for m in range(2):
-                block = (meta[2 * reqs + 1] + m) % 2 * ring + (meta[2 * reqs + 2] - n + ring) % ring
-                q_all[pl.ds(pl.multiple_of(block * TB, TB), TB), :] = pair[m * TB:(m + 1) * TB, :]
     of_head = lax.broadcasted_iota(jnp.int32, (TB, HD), 1) % heads
     token = lax.broadcasted_iota(jnp.int32, (1, lanes), 1) % TB
     key = lax.broadcasted_iota(jnp.int32, (KC, lanes), 0)
 
-    @pl.loop(tiles, NEWQ // TB)
-    def _(i):
-        row = pl.multiple_of(i * TB, TB)
-        o_ref[pl.ds(row, TB), :width] = jnp.zeros((TB, width), o_ref.dtype)
-        o_ref[pl.ds(row, TB), width:] = pack_logs(jnp.full((TB, HD), HIDDEN, jnp.float32), heads)
+    def block(j):
+        across, along = lax.rem(j, 2), lead + j // 2
+        return (meta[2 * reqs + 1] + across) % 2 * ring + (meta[2 * reqs + 2] - along + ring) % ring
+
+    def spot(j):
+        return pl.ds(pl.multiple_of((block(j) if lead else j) * TB, TB), TB)
+
+    def note(j, tiles):
+        take = some & (block(j) * TB < new_count)
+
+        @pl.when(take)
+        def _():
+            order[tiles] = j
+
+        @pl.when(jnp.logical_not(take))
+        def _():
+            none = jnp.full((TB, HD), HIDDEN, jnp.float32)
+            o_ref[place, spot(j), :width] = jnp.zeros((TB, width), o_ref.dtype)
+            o_ref[place, spot(j), width:] = pack_logs(none, heads)
+
+        return tiles + take.astype(jnp.int32)
+
+    tiles = lax.fori_loop(0, count, note, jnp.int32(0))
 
     def step(i, span, clear):
-        row = pl.multiple_of(jnp.minimum(i, tiles - 1) * TB, TB)
+        tile = order[jnp.minimum(i, tiles - 1)]
+        row = pl.multiple_of(tile * TB, TB)
         q = jnp.concatenate(
-            [q_ref[pl.ds(row, TB), h * HD:(h + 1) * HD] for h in range(heads)], axis=0)
-        shown = edge + row + token
+            [q_ref[place, pl.ds(row, TB), h * HD:(h + 1) * HD] for h in range(heads)], axis=0)
+        shown = edge + block(tile) * TB + token
         shift = jnp.max(mx[...], axis=0, keepdims=True) * RATE
         top = acc = total = None
         for c in range(span):
             at = slice(c * KC, (c + 1) * KC)
             e = jnp.exp2(s[at, :] * RATE - shift)
-            part = lax.dot_general(k_ref[at, :], q, (((1,), (1,)), ((), ())),
+            part = lax.dot_general(k_ref[req, at, :], q, (((1,), (1,)), ((), ())),
                                    preferred_element_type=jnp.float32)
             if c >= clear:
                 part = jnp.where(key < shown - c * KC, part, HIDDEN)
@@ -75,30 +86,24 @@
             top = high if top is None else jnp.maximum(top, high)
             add = jnp.sum(e.reshape(KC // 8, 8, lanes), axis=0)
             total = add if total is None else total + add
-            new = jnp.dot(vt_ref[:, at], e.astype(jnp.bfloat16), preferred_element_type=jnp.float32)
+            new = jnp.dot(vt_ref[req, :, at], e.astype(jnp.bfloat16), preferred_element_type=jnp.float32)
             acc = new if acc is None else acc + new
         mx[...] = top
-        row = pl.multiple_of(jnp.maximum(i - 1, 0) * TB, TB)
+        there = spot(order[jnp.maximum(i - 1, 0)])
         total = jnp.sum(total, axis=0, keepdims=True)
         out = (acc / total).T
         ls = jnp.broadcast_to(shift + jnp.log2(total), (HD, lanes)).T
         kept = jnp.zeros((TB, HD), jnp.float32)
         for h in range(heads):
             at = slice(h * TB, (h + 1) * TB)
-            o_ref[pl.ds(row, TB), h * HD:(h + 1) * HD] = out[at].astype(o_ref.dtype)
+            o_ref[place, there, h * HD:(h + 1) * HD] = out[at].astype(o_ref.dtype)
             kept = jnp.where(of_head == h, ls[at], kept)
-        o_ref[pl.ds(row, TB), width:] = pack_logs(kept, heads)
-
-    def run(span, clear):
-        @pl.loop(0, tiles + 1)
-        def _(i):
-            step(i, span, clear)
+        o_ref[place, there, width:] = pack_logs(kept, heads)
 
     chunks = slots // KC
     cuts = (0, 3, 7, 10, chunks - 1, chunks)
     for low, high in zip(cuts, cuts[1:] + (None,)):
         span = chunks if high is None else min(chunks, high + NEWQ // KC)
-        clear = low
         here = tiles > 0
         if low > 0:
             here = here & (edge >= low * KC)
@@ -106,61 +111,90 @@
             here = here & (edge < high * KC)
 
         @pl.when(here)
-        def _(span=span, clear=clear):
-            run(span, clear)
-
-
-def attend(req, meta, qs, k, vt):
-    rows, width = NEWQ, qs[0].shape[1]
-    slots = k.shape[0]
-    heads = width // HD
+        def _(span=span, clear=low):
+            @pl.loop(0, tiles + 1)
+            def _(i):
+                step(i, span, clear)
+
+    return block
+
+
+def own_kernel(meta, q_ref, k_ref, vt_ref, o_ref, s, mx, order):
+    @pl.loop(0, q_ref.shape[0])
+    def _(r):
+        sweep(r, r, 0, meta, q_ref, k_ref, vt_ref, o_ref, s, mx, order)
+
+
+def rest_kernel(req, meta, done_ref, *refs):
+    *q_refs, k_ref, vt_ref, o_ref, s, mx, order, q_all = refs
+    rows = 2 * TB
+    for n, pair in enumerate(q_refs):
+        q_all[0, n * rows:(n + 1) * rows, :] = pair[...]
+    block = sweep(req, 0, 1, meta, q_all, k_ref, vt_ref, o_ref, s, mx, order)
+    for m in range(2):
+        at = pl.ds(pl.multiple_of(block(jnp.int32(m - 2)) * TB, TB), TB)
+        o_ref[0, at, :] = done_ref[req, m * TB:(m + 1) * TB, :]
+
+
+def attend(req, meta, qs, keys, turned, done=None):
+    width = qs[0].shape[-1]
+    slots = keys.shape[1]
+    lanes = width // HD * TB
+    scratch = [
+        pltpu.VMEM((slots, lanes), jnp.float32),
+        pltpu.VMEM((8, lanes), jnp.float32),
+        pltpu.SMEM((NEWQ // TB,), jnp.int32),
+    ]
+    if done is None:
+        body, shape, extra = own_kernel, qs[0].shape[:2], []
+        tiles = shape[0] * 2
+    else:
+        body, shape, extra = functools.partial(rest_kernel, req), (1, NEWQ), [done]
+        tiles = 2 * len(qs)
+        scratch.append(pltpu.VMEM((1, tiles * TB, width), jnp.bfloat16))
     return pl.pallas_call(
-        functools.partial(attend_kernel, req),
-        out_shape=jax.ShapeDtypeStruct((rows, width + HD), jnp.bfloat16),
-        in_specs=[SMEM] + [VMEM] * (len(qs) + 2),
+        body,
+        out_shape=jax.ShapeDtypeStruct(shape + (width + HD,), jnp.bfloat16),
+        in_specs=[SMEM] + [VMEM] * (len(extra) + len(qs) + 2),
         out_specs=VMEM,
-        scratch_shapes=[
-            pltpu.VMEM((slots, heads * TB), jnp.float32),
-            pltpu.VMEM((8, heads * TB), jnp.float32),
-            pltpu.VMEM((rows if len(qs) > 1 else TB, width), jnp.bfloat16),
-        ],
+        scratch_shapes=scratch,
         compiler_params=pltpu.CompilerParams(vmem_limit_bytes=40 * 2**20),
         cost_estimate=pl.CostEstimate(
-            flops=8 * rows * heads * slots * HD, bytes_accessed=4 * 2**20,
-            transcendentals=rows * heads * slots),
-    )(meta, *qs, k, vt)
-
-
-def part_kernel(k_ref, v_ref, *refs):
-    reqs = (len(refs) - 1) // 2
-    scratch = refs[-1]
-    n = k_ref.shape[0] // reqs
-    scratch[0] = k_ref[...].astype(jnp.float32)
-    scratch[1] = v_ref[...].astype(jnp.float32)
+            flops=8 * tiles * lanes * slots * HD, bytes_accessed=4 * 2**20,
+            transcendentals=tiles * lanes * slots),
+    )(meta, *extra, *qs, keys, turned)
+
+
+def part_kernel(k_ref, v_ref, keys_ref, turned_ref, flat):
+    reqs, n, _ = keys_ref.shape
+    flat[0] = k_ref[...].astype(jnp.float32)
+    flat[1] = v_ref[...].astype(jnp.float32)
     for r in range(reqs):
-        refs[r][...] = scratch[0, pl.ds(r, n, stride=reqs), :].astype(jnp.bfloat16)
-        refs[reqs + r][...] = scratch[1, pl.ds(r, n, stride=reqs), :].T.astype(jnp.bfloat16)
+        keys_ref[r] = flat[0, pl.ds(r, n, stride=reqs), :].astype(jnp.bfloat16)
+        turned_ref[r] = flat[1, pl.ds(r, n, stride=reqs), :].T.astype(jnp.bfloat16)
 
 
 def part_caches(keys, values):
     slots, reqs, _ = keys.shape
     n = 512
     flat = pl.BlockSpec((n * reqs, HD), lambda i: (i, 0))
-    shape = jax.ShapeDtypeStruct((slots, HD), jnp.bfloat16)
-    turned = jax.ShapeDtypeStruct((HD, slots), jnp.bfloat16)
-    outs = pl.pallas_call(
+    return pl.pallas_call(
         part_kernel,
         grid=(slots // n,),
-        out_shape=[shape] * reqs + [turned] * reqs,
+        out_shape=[
+            jax.ShapeDtypeStruct((reqs, slots, HD), jnp.bfloat16),
+            jax.ShapeDtypeStruct((reqs, HD, slots), jnp.bfloat16),
+        ],
         in_specs=[flat, flat],
-        out_specs=[pl.BlockSpec((n, HD), lambda i: (i, 0))] * reqs
-        + [pl.BlockSpec((HD, n), lambda i: (0, i))] * reqs,
+        out_specs=[
+            pl.BlockSpec((reqs, n, HD), lambda i: (0, i, 0)),
+            pl.BlockSpec((reqs, HD, n), lambda i: (0, 0, i)),
+        ],
         scratch_shapes=[pltpu.VMEM((2, n * reqs, HD), jnp.float32)],
         compiler_params=pltpu.CompilerParams(vmem_limit_bytes=16 * 2**20),
         cost_estimate=pl.CostEstimate(
             flops=0, bytes_accessed=8 * keys.size, transcendentals=0),
     )(keys.reshape(slots * reqs, HD), values.reshape(slots * reqs, HD))
-    return outs[:reqs], outs[reqs:]
 
 
 def merge_kernel(req, meta, part_ref, out_ref, *, cycle, heads):
@@ -230,9 +264,10 @@
     other, meta, (keys, turned) = lax.optimization_barrier((shifted(split, 1, 0), meta, caches))
     pairs = jnp.concatenate([split, other], axis=1)
     outs = []
+    done = attend(None, meta, [pairs], keys, turned)
     for r in range(reqs):
-        qs = [pairs[r]] + [shifted(pairs[r], 0, n) for n in range(1, ring)]
-        part = attend(r, meta, qs, keys[r], turned[r])
+        qs = [shifted(pairs[r], 0, n) for n in range(1, ring)]
+        part = attend(r, meta, qs, keys, turned, done)
         part = part.reshape(owners, tok_rows, width + HD)
         part = lax.all_to_all(part, ("ctx", "tp"), split_axis=0, concat_axis=0)
         outs.append(merge(r, meta, part, cycle, heads))

time: 104 us -> 101 us (0.971)
  the two profiles are of different devices: /device:TPU:0 before, /device:TPU:1 now
where the time goes in v2:
time: 101 us; the launch traced here: 102 us
  Pallas kernels  45.5 us (45%)
  starting transfers between devices  30.1 us (30%)
  waiting for transfers between devices  17.6 us (17%)
  local copies, waits for them, and re-layouts  8.89 us (9%)
    pallas_call x3, Pallas kernels, attend(): pl.pallas_call(body, out_shape=jax.ShapeDtypeStruct(shape + (width + HD,)...  40.3 us
    all_to_all x2, starting transfers between devices, shards(): part = lax.all_to_all(part, ('ctx', 'tp'), split_axis=0, concat_axis=0)  17.3 us
    all_to_all x2, waiting for transfers between devices, shards(): part = lax.all_to_all(part, ('ctx', 'tp'), split_axis=0, concat_axis=0)  17.3 us
    ppermute x7, starting transfers between devices, shifted(): return lax.ppermute(block, 'ctx', route)  12.8 us
    unnamed x19, local copies, waits for them, and re-layouts  7.83 us
    pallas_call x2, Pallas kernels, merge(): pl.pallas_call(functools.partial(merge_kernel, req, cycle=cycle, heads=he...  3.84 us
  transfers between devices with their start and end apart: 9, of which 2 were waited for; matrix products, arithmetic and copies ran while one was open for 0% of the time, Pallas kernels for 43%

profile of v2, /device:TPU:1, one launch (start us, length us, event | category | flops | bytes accessed | tf_op | source)
XLA Modules:
  0.0 102.3 jit_solution(15719017596773301600)
XLA Ops:
  0.0 1.0 %copy.9 = bf16[32,2,2048]{2,0,1:T(8,128)(2,1)S(1)} copy(bf16[32,2,2048]{2,1,0:T(2,128)(2,1)} %param.5) | data formatting | bytes 524288 | tf_op args[0]
  1.0 3.8 %collective-permute-start = (bf16[2,32,2048]{2,1,0:T(8,128)(2,1)S(1)}, bf16[2,32,2048]{2,1,0:T(8,128)(2,1)S(1)}, u32[]{:S(2)}, u32[]{:S(2)}) collective-permute-start(bf16[2,32,2048]{2,1,0:T(8,128)(2,1)S(1)} %bitcast.21), channel_id=1, source_target_pairs={{0,64},{16,80},{32,96},{48,112},{64,0},{80,16},{96,32},{112,48},{1... | collective-permute-start | bytes 786440 | tf_op jit(solution)/shard_map/ppermute | solution.py:246
  4.9 0.0 copy-start
  4.9 1.4 %copy-done = bf16[3072,2,128]{2,1,0:T(2,128)(2,1)S(1)} copy-done((bf16[3072,2,128]{2,1,0:T(2,128)(2,1)S(1)}, bf16[3072,2,128]{2,1,0:T(2,128)(2,1)}, u32[]{:S(2)}) %copy-start) | copy-done | bytes 1572888
  6.3 0.0 copy-start.1
  6.3 1.4 %copy-done.1 = bf16[3072,2,128]{2,1,0:T(2,128)(2,1)S(1)} copy-done((bf16[3072,2,128]{2,1,0:T(2,128)(2,1)S(1)}, bf16[3072,2,128]{2,1,0:T(2,128)(2,1)}, u32[]{:S(2)}) %copy-start.1) | copy-done | bytes 1572888
  7.7 0.0 copy-start.7
  7.7 0.0 copy-start.8
  7.7 1.4 %shard_map.55 = (bf16[2,3072,128]{2,1,0:T(8,128)(2,1)S(1)}, bf16[2,128,3072]{2,1,0:T(8,128)(2,1)S(1)}) custom-call(bf16[6144,128]{1,0:T(8,128)(2,1)S(1)} %bitcast.19, bf16[6144,128]{1,0:T(8,128)(2,1)S(1)} %bitcast.20), custom_call_target="tpu_custom_call" | custom-call | bytes 6291456 | tf_op jit(solution)/shard_map/pallas_call | solution.py:181
  9.1 0.0 copy-start.4
  9.1 1.2 %copy-done.4 = bf16[2,128,3072]{2,1,0:T(8,128)(2,1)} copy-done((bf16[2,128,3072]{2,1,0:T(8,128)(2,1)}, bf16[2,128,3072]{2,1,0:T(8,128)(2,1)S(1)}, u32[]{:S(2)}) %copy-start.4) | copy-done | bytes 1572888
  10.3 0.0 copy-start.2
  10.3 0.0 copy-done.7
  10.3 0.0 copy-done.8
  10.3 0.1 concatenate.6.meta
  10.4 0.0 copy-start.5
  10.4 0.2 collective-permute-done
  10.7 1.7 %collective-permute-start.1 = (bf16[64,2048]{1,0:T(8,128)(2,1)S(1)}, bf16[64,2048]{1,0:T(8,128)(2,1)S(1)}, u32[]{:S(2)}, u32[]{:S(2)}) collective-permute-start(bf16[64,2048]{1,0:T(8,128)(2,1)S(1)} %get-tuple-element.17), channel_id=1, source_target_pairs={{0,16},{16,32},{32,48},{48,0},{64,80},{80,96},{96,112},{112,64},{1... | collective-permute-start | bytes 786440 | tf_op jit(solution)/shard_map/ppermute | solution.py:246
  12.4 3.3 %collective-permute-start.2 = (bf16[64,2048]{1,0:T(8,128)(2,1)S(1)}, bf16[64,2048]{1,0:T(8,128)(2,1)S(1)}, u32[]{:S(2)}, u32[]{:S(2)}) collective-permute-start(bf16[64,2048]{1,0:T(8,128)(2,1)S(1)} %get-tuple-element.17), channel_id=1, source_target_pairs={{0,32},{16,48},{32,0},{48,16},{64,96},{80,112},{96,64},{112,80},{1... | collective-permute-start | bytes 786440 | tf_op jit(solution)/shard_map/ppermute | solution.py:246
  15.7 0.7 collective-permute-start.3
  16.4 0.7 collective-permute-start.4
  17.2 0.4 collective-permute-start.5
  17.6 0.0 copy-done.5
  17.6 11.4 %shard_map.56.done_ref = bf16[2,64,2176]{2,1,0:T(8,128)(2,1)S(1)} custom-call(s32[8]{0:T(128)S(1)} %concatenate.6.meta, bf16[2,64,2048]{2,1,0:T(8,128)(2,1)S(1)} %pad_maximum_fusion.q_ref, bf16[2,3072,128]{2,1,0:T(8,128)(2,1)S(1)} %get-tuple-element.15.k_ref.refs_3_, bf16[2,128,3072]{2,1,0:T(8,128)(2,1)S(1)} %copy-done.5), custom_call_target="tpu_custom_call" | custom-call | flops 6442450944 | bytes 4194304 | tf_op jit(solution)/shard_map/pallas_call | solution.py:155
  29.0 0.0 collective-permute-done.1.refs_0_
  29.1 2.0 %collective-permute-start.6 = (bf16[64,2048]{1,0:T(8,128)(2,1)S(1)}, bf16[64,2048]{1,0:T(8,128)(2,1)S(1)}, u32[]{:S(2)}, u32[]{:S(2)}) collective-permute-start(bf16[64,2048]{1,0:T(8,128)(2,1)S(1)} %get-tuple-element.18), channel_id=1, source_target_pairs={{0,48},{16,0},{32,16},{48,32},{64,112},{80,64},{96,80},{112,96},{1... | collective-permute-start | bytes 786440 | tf_op jit(solution)/shard_map/ppermute | solution.py:246
  31.1 0.0 collective-permute-done.2.refs_1_
  31.1 0.0 collective-permute-done.3.refs_2_
  31.1 0.0 copy-done.2
  31.1 14.4 %shard_map.57 = bf16[1,256,2176]{2,1,0:T(8,128)(2,1)} custom-call(s32[8]{0:T(128)S(1)} %concatenate.6.meta, bf16[2,64,2176]{2,1,0:T(8,128)(2,1)S(1)} %shard_map.56.done_ref, bf16[64,2048]{1,0:T(8,128)(2,1)S(1)} %collective-permute-done.1.refs_0_, bf16[64,2048]{1,0:T(8,128)(2,1)S(1)} %collective-permute-done.2.refs_1_, ...), custom_call_target="tpu_custom_call" | custom-call | flops 9663676416 | bytes 4194304 | tf_op jit(solution)/shard_map/pallas_call | solution.py:155
  45.5 8.1 %all-to-all-start = ((bf16[32,8,2176]{2,1,0:T(8,128)(2,1)}), bf16[32,8,2176]{2,1,0:T(8,128)(2,1)S(1)}, u32[]{:S(2)}, u32[]{:S(2)}) async-start(bf16[32,8,2176]{2,1,0:T(8,128)(2,1)} %bitcast.8), calls=%async_computation | async-start | bytes 2228224 | tf_op jit(solution)/shard_map/all_to_all | solution.py:272
  53.5 0.0 collective-permute-done.4.refs_0_
  53.6 0.0 collective-permute-done.5.refs_1_
  53.6 0.0 collective-permute-done.6.refs_2_
  53.6 0.0 copy-start.3
  53.6 1.4 %copy-done.3 = bf16[2,3072,128]{2,1,0:T(8,128)(2,1)S(1)} copy-done((bf16[2,3072,128]{2,1,0:T(8,128)(2,1)S(1)}, bf16[2,3072,128]{2,1,0:T(8,128)(2,1)}, u32[]{:S(2)}) %copy-start.3) | copy-done | bytes 1572888
  55.0 0.0 copy-start.6
  55.0 1.4 %copy-done.6 = bf16[2,128,3072]{2,1,0:T(8,128)(2,1)S(1)} copy-done((bf16[2,128,3072]{2,1,0:T(8,128)(2,1)S(1)}, bf16[2,128,3072]{2,1,0:T(8,128)(2,1)}, u32[]{:S(2)}) %copy-start.6) | copy-done | bytes 1572888
  56.4 14.5 %shard_map.59 = bf16[1,256,2176]{2,1,0:T(8,128)(2,1)} custom-call(s32[8]{0:T(128)S(1)} %concatenate.6.meta, bf16[2,64,2176]{2,1,0:T(8,128)(2,1)S(1)} %shard_map.56.done_ref, bf16[64,2048]{1,0:T(8,128)(2,1)S(1)} %collective-permute-done.4.refs_0_, bf16[64,2048]{1,0:T(8,128)(2,1)S(1)} %collective-permute-done.5.refs_1_, ...), custom_call_target="tpu_custom_call" | custom-call | flops 9663676416 | bytes 4194304 | tf_op jit(solution)/shard_map/pallas_call | solution.py:155
  70.9 0.0 all-to-all-done.part_ref
  70.9 9.3 %all-to-all-start.1 = ((bf16[32,8,2176]{2,1,0:T(8,128)(2,1)}), bf16[32,8,2176]{2,1,0:T(8,128)(2,1)S(1)}, u32[]{:S(2)}, u32[]{:S(2)}) async-start(bf16[32,8,2176]{2,1,0:T(8,128)(2,1)} %bitcast.11), calls=%async_computation.1 | async-start | bytes 2228224 | tf_op jit(solution)/shard_map/all_to_all | solution.py:272
  80.1 1.9 %shard_map.58 = f32[8,8192]{1,0:T(8,128)S(1)} custom-call(s32[8]{0:T(128)S(1)} %concatenate.6.meta, bf16[32,8,2176]{2,1,0:T(8,128)(2,1)S(1)} %all-to-all-done.part_ref), custom_call_target="tpu_custom_call" | custom-call | flops 1114112 | bytes 1114112 | tf_op jit(solution)/shard_map/pallas_call | solution.py:229
  82.1 17.3 %all-to-all-done.1.part_ref = bf16[32,8,2176]{2,1,0:T(8,128)(2,1)S(1)} async-done(((bf16[32,8,2176]{2,1,0:T(8,128)(2,1)}), bf16[32,8,2176]{2,1,0:T(8,128)(2,1)S(1)}, u32[]{:S(2)}, u32[]{:S(2)}) %all-to-all-start.1) | async-done | bytes 1114144 | tf_op jit(solution)/shard_map/all_to_all | solution.py:272
  99.4 1.9 %shard_map.60 = f32[8,8192]{1,0:T(8,128)S(1)} custom-call(s32[8]{0:T(128)S(1)} %concatenate.6.meta, bf16[32,8,2176]{2,1,0:T(8,128)(2,1)S(1)} %all-to-all-done.1.part_ref), custom_call_target="tpu_custom_call" | custom-call | flops 1114112 | bytes 1114112 | tf_op jit(solution)/shard_map/pallas_call | solution.py:229
  101.4 1.0 copy.7
  (5 shorter events, 0.1 us)
Async XLA Ops:
  1.0 9.6 %collective-permute-start = (bf16[2,32,2048]{2,1,0:T(8,128)(2,1)S(1)}, bf16[2,32,2048]{2,1,0:T(8,128)(2,1)S(1)}, u32[]{:S(2)}, u32[]{:S(2)}) collective-permute-start(bf16[2,32,2048]{2,1,0:T(8,128)(2,1)S(1)} %bitcast.21), channel_id=1, source_target_pairs={{0,64},{16,80},{32,96},{48,112},{64,0},{80,16},{96,32},{112,48},{1... | collective-permute-start | bytes 786440 | tf_op jit(solution)/shard_map/ppermute | solution.py:246
  4.9 1.4 %copy-start = (bf16[3072,2,128]{2,1,0:T(2,128)(2,1)S(1)}, bf16[3072,2,128]{2,1,0:T(2,128)(2,1)}, u32[]{:S(2)}) copy-start(bf16[3072,2,128]{2,1,0:T(2,128)(2,1)} %param.6) | copy-start | bytes 4718596
  6.3 1.4 %copy-start.1 = (bf16[3072,2,128]{2,1,0:T(2,128)(2,1)S(1)}, bf16[3072,2,128]{2,1,0:T(2,128)(2,1)}, u32[]{:S(2)}) copy-start(bf16[3072,2,128]{2,1,0:T(2,128)(2,1)} %param.7) | copy-start | bytes 4718596
  7.7 2.6 %copy-start.7 = (s32[2]{0:T(128)S(1)}, s32[2]{0:T(128)}, u32[]{:S(2)}) copy-start(s32[2]{0:T(128)} %param.8) | copy-start | bytes 28
  7.7 2.6 %copy-start.8 = (s32[2]{0:T(128)S(1)}, s32[2]{0:T(128)}, u32[]{:S(2)}) copy-start(s32[2]{0:T(128)} %param.9) | copy-start | bytes 28
  9.1 1.2 %copy-start.4 = (bf16[2,128,3072]{2,1,0:T(8,128)(2,1)}, bf16[2,128,3072]{2,1,0:T(8,128)(2,1)S(1)}, u32[]{:S(2)}) copy-start(bf16[2,128,3072]{2,1,0:T(8,128)(2,1)S(1)} %get-tuple-element.16.vt_ref.refs_4_) | copy-start | bytes 4718596
  10.3 20.8 %copy-start.2 = (bf16[2,3072,128]{2,1,0:T(8,128)(2,1)}, bf16[2,3072,128]{2,1,0:T(8,128)(2,1)S(1)}, u32[]{:S(2)}) copy-start(bf16[2,3072,128]{2,1,0:T(8,128)(2,1)S(1)} %get-tuple-element.15.k_ref.refs_3_) | copy-start | bytes 4718596
  10.4 7.2 %copy-start.5 = (bf16[2,128,3072]{2,1,0:T(8,128)(2,1)S(1)}, bf16[2,128,3072]{2,1,0:T(8,128)(2,1)}, u32[]{:S(2)}) copy-start(bf16[2,128,3072]{2,1,0:T(8,128)(2,1)} %copy-done.4) | copy-start | bytes 4718596
  10.7 18.4 %collective-permute-start.1 = (bf16[64,2048]{1,0:T(8,128)(2,1)S(1)}, bf16[64,2048]{1,0:T(8,128)(2,1)S(1)}, u32[]{:S(2)}, u32[]{:S(2)}) collective-permute-start(bf16[64,2048]{1,0:T(8,128)(2,1)S(1)} %get-tuple-element.17), channel_id=1, source_target_pairs={{0,16},{16,32},{32,48},{48,0},{64,80},{80,96},{96,112},{112,64},{1... | collective-permute-start | bytes 786440 | tf_op jit(solution)/shard_map/ppermute | solution.py:246
  12.4 18.7 %collective-permute-start.2 = (bf16[64,2048]{1,0:T(8,128)(2,1)S(1)}, bf16[64,2048]{1,0:T(8,128)(2,1)S(1)}, u32[]{:S(2)}, u32[]{:S(2)}) collective-permute-start(bf16[64,2048]{1,0:T(8,128)(2,1)S(1)} %get-tuple-element.17), channel_id=1, source_target_pairs={{0,32},{16,48},{32,0},{48,16},{64,96},{80,112},{96,64},{112,80},{1... | collective-permute-start | bytes 786440 | tf_op jit(solution)/shard_map/ppermute | solution.py:246
  15.7 15.4 %collective-permute-start.3 = (bf16[64,2048]{1,0:T(8,128)(2,1)S(1)}, bf16[64,2048]{1,0:T(8,128)(2,1)S(1)}, u32[]{:S(2)}, u32[]{:S(2)}) collective-permute-start(bf16[64,2048]{1,0:T(8,128)(2,1)S(1)} %get-tuple-element.17), channel_id=1, source_target_pairs={{0,48},{16,0},{32,16},{48,32},{64,112},{80,64},{96,80},{112,96},{1... | collective-permute-start | bytes 786440 | tf_op jit(solution)/shard_map/ppermute | solution.py:246
  16.4 37.1 %collective-permute-start.4 = (bf16[64,2048]{1,0:T(8,128)(2,1)S(1)}, bf16[64,2048]{1,0:T(8,128)(2,1)S(1)}, u32[]{:S(2)}, u32[]{:S(2)}) collective-permute-start(bf16[64,2048]{1,0:T(8,128)(2,1)S(1)} %get-tuple-element.18), channel_id=1, source_target_pairs={{0,16},{16,32},{32,48},{48,0},{64,80},{80,96},{96,112},{112,64},{1... | collective-permute-start | bytes 786440 | tf_op jit(solution)/shard_map/ppermute | solution.py:246
  17.2 36.4 %collective-permute-start.5 = (bf16[64,2048]{1,0:T(8,128)(2,1)S(1)}, bf16[64,2048]{1,0:T(8,128)(2,1)S(1)}, u32[]{:S(2)}, u32[]{:S(2)}) collective-permute-start(bf16[64,2048]{1,0:T(8,128)(2,1)S(1)} %get-tuple-element.18), channel_id=1, source_target_pairs={{0,32},{16,48},{32,0},{48,16},{64,96},{80,112},{96,64},{112,80},{1... | collective-permute-start | bytes 786440 | tf_op jit(solution)/shard_map/ppermute | solution.py:246
  29.1 24.5 %collective-permute-start.6 = (bf16[64,2048]{1,0:T(8,128)(2,1)S(1)}, bf16[64,2048]{1,0:T(8,128)(2,1)S(1)}, u32[]{:S(2)}, u32[]{:S(2)}) collective-permute-start(bf16[64,2048]{1,0:T(8,128)(2,1)S(1)} %get-tuple-element.18), channel_id=1, source_target_pairs={{0,48},{16,0},{32,16},{48,32},{64,112},{80,64},{96,80},{112,96},{1... | collective-permute-start | bytes 786440 | tf_op jit(solution)/shard_map/ppermute | solution.py:246
  45.5 25.4 %all-to-all-start = ((bf16[32,8,2176]{2,1,0:T(8,128)(2,1)}), bf16[32,8,2176]{2,1,0:T(8,128)(2,1)S(1)}, u32[]{:S(2)}, u32[]{:S(2)}) async-start(bf16[32,8,2176]{2,1,0:T(8,128)(2,1)} %bitcast.8), calls=%async_computation | async-start | bytes 2228224 | tf_op jit(solution)/shard_map/all_to_all | solution.py:272
  53.6 1.4 %copy-start.3 = (bf16[2,3072,128]{2,1,0:T(8,128)(2,1)S(1)}, bf16[2,3072,128]{2,1,0:T(8,128)(2,1)}, u32[]{:S(2)}) copy-start(bf16[2,3072,128]{2,1,0:T(8,128)(2,1)} %copy-done.2) | copy-start | bytes 4718596
  55.0 1.4 %copy-start.6 = (bf16[2,128,3072]{2,1,0:T(8,128)(2,1)S(1)}, bf16[2,128,3072]{2,1,0:T(8,128)(2,1)}, u32[]{:S(2)}) copy-start(bf16[2,128,3072]{2,1,0:T(8,128)(2,1)} %copy-done.4) | copy-start | bytes 4718596
  70.9 28.5 %all-to-all-start.1 = ((bf16[32,8,2176]{2,1,0:T(8,128)(2,1)}), bf16[32,8,2176]{2,1,0:T(8,128)(2,1)S(1)}, u32[]{:S(2)}, u32[]{:S(2)}) async-start(bf16[32,8,2176]{2,1,0:T(8,128)(2,1)} %bitcast.11), calls=%async_computation.1 | async-start | bytes 2228224 | tf_op jit(solution)/shard_map/all_to_all | solution.py:272
